TPU v7x, 32 devices: a whole 2x2x4 slice. The times are simulated.
32 devices in a mesh: groups: 2 (over x), tm: 16 (over z, y, core).
Axes of the slice: x: 2, y: 2, z: 4, core: 2. Of those that a mesh axis runs over, the one named last changes fastest.
Arguments:
- inputs: bfloat16 [32768, 1536], P(('groups', 'tm')), parts along dimension 0
- counts: int32 [32], P(('groups', 'tm')), parts along dimension 0, may hold values from 1 to 1024, as said below
- query_weight: bfloat16 [1536, 1024], replicated
- key_weight: bfloat16 [1536, 1024], replicated
- value_weight: bfloat16 [1536, 1024], replicated, may hold values from -0.625 to 0.625
Outputs:
- attended: bfloat16 [32768, 1024], P(('groups', 'tm')), parts along dimension 0
There are 2 independent parts, one for each index of `groups`. A program takes and returns all parts, laid end to end along the dimension named above; an argument that names none is the same for every part. Nothing has to cross between parts.
Inputs may be any that keep to these rules, and one draw needn't show every extreme that they name: `counts`: each entry is the number of valid frames at the start of that index's 1024 frames; at least one entry equals 1024.
All inputs are finite; a program needn't handle non-finite values.
Results may differ from a plain program's by a relative error of at most 0.0085.
Values may be sent and summed in bfloat16 or wider, within the bound.
A program may use at most 192 MiB of HBM per device.

v0:
```python
import functools

import jax
import jax.numpy as jnp
from jax import lax
from jax.experimental import pallas as pl
from jax.experimental.pallas import tpu as pltpu
from jax.sharding import PartitionSpec as P

DH = 64
WINDOW = 128
PAIR = 2 * DH
SPAN = 3 * WINDOW
LOG2E = 1.4426950408889634
MESH = pl.DeviceIdType.MESH
NT = (((1,), (1,)), ((), ()))


def normalize(rows):
    values = rows.astype(jnp.float32)
    average = jnp.mean(values, axis=-1, keepdims=True)
    centred = values - average
    spread = jnp.mean(centred * centred, axis=-1, keepdims=True)
    return (centred * lax.rsqrt(spread + 1e-05)).astype(jnp.bfloat16)


def kernel(
    counts, x_hbm, wq_hbm, wk_hbm, wv_hbm, out_hbm,
    x, wq, wk, wv, q, k, v, o, bias, cnt, cnt_near,
    x_sem, w_sem, out_sem, send_sem, recv_sem,
):
    rows, width = out_hbm.shape
    blocks = rows // WINDOW
    tm = lax.axis_size("tm")
    me = lax.axis_index("tm")
    has_left, has_right = me > 0, me < tm - 1
    barrier = pltpu.get_barrier_semaphore()

    @pl.when(has_left)
    def _():
        pl.semaphore_signal(barrier, inc=1, device_id={"tm": me - 1}, device_id_type=MESH)

    @pl.when(has_right)
    def _():
        pl.semaphore_signal(barrier, inc=1, device_id={"tm": me + 1}, device_id_type=MESH)

    chunk = 256
    x_copy = [
        pltpu.make_async_copy(
            x_hbm.at[pl.ds(c * chunk, chunk)], x.at[pl.ds(c * chunk, chunk)], x_sem.at[c]
        )
        for c in range(rows // chunk)
    ]
    w_copy = [
        pltpu.make_async_copy(src, dst, w_sem.at[n])
        for n, (src, dst) in enumerate(((wk_hbm, wk), (wv_hbm, wv), (wq_hbm, wq)))
    ]
    for copy in x_copy + w_copy:
        copy.start()
    cnt[...] = jnp.full(cnt.shape, counts[0], jnp.int32)

    def remote(n, src, dst, to):
        return pltpu.make_async_remote_copy(
            src_ref=src, dst_ref=dst, send_sem=send_sem.at[n], recv_sem=recv_sem.at[n],
            device_id={"tm": to}, device_id_type=MESH,
        )

    first, last = pl.ds(WINDOW, WINDOW), pl.ds(rows, WINDOW)
    before, after = pl.ds(0, WINDOW), pl.ds(rows + WINDOW, WINDOW)
    to_right = [
        remote(0, cnt, cnt_near.at[0], me + 1),
        remote(1, k.at[last], k.at[before], me + 1),
        remote(2, v.at[last], v.at[before], me + 1),
    ]
    to_left = [
        remote(3, cnt, cnt_near.at[1], me - 1),
        remote(4, k.at[first], k.at[after], me - 1),
        remote(5, v.at[first], v.at[after], me - 1),
    ]

    def send(n):
        @pl.when(has_right)
        def _():
            to_right[n].start()

        @pl.when(has_left)
        def _():
            to_left[n].start()

    for c in range(rows // chunk):
        x_copy[c].wait()

        def norm(t, carry, c=c):
            part = pl.ds(pl.multiple_of(c * chunk + t * 64, 64), 64)
            x[part] = normalize(x[part])
            return carry

        lax.fori_loop(0, chunk // 64, norm, 0)

    def project(w, dst, shift, scale):
        def step(t, carry):
            col = pl.ds(pl.multiple_of((t // 2) * 256, 256), 256)
            at = (t % 2) * (rows // 2)
            src = pl.ds(pl.multiple_of(at, 256), rows // 2)
            to = pl.ds(pl.multiple_of(at + shift, 128), rows // 2)
            y = jnp.dot(x[src], w[:, col], preferred_element_type=jnp.float32)
            if scale != 1.0:
                y = y * scale
            dst[to, col] = y.astype(jnp.bfloat16)
            return carry

        lax.fori_loop(0, 2 * (width // 256), step, 0)

    w_copy[0].wait()
    project(wk, k, WINDOW, 1.0)

    pl.semaphore_wait(barrier, has_left.astype(jnp.int32) + has_right.astype(jnp.int32))
    send(0)
    send(1)
    w_copy[1].wait()
    project(wv, v, WINDOW, 1.0)
    send(2)
    w_copy[2].wait()
    project(wq, q, 0, DH ** (-0.5) * LOG2E)

    row = lax.broadcasted_iota(jnp.int32, (WINDOW, SPAN), 0)
    lane = lax.broadcasted_iota(jnp.int32, (WINDOW, SPAN), 1)
    offset = lane - WINDOW - row
    head_a = lax.broadcasted_iota(jnp.int32, (WINDOW, PAIR), 1) < DH
    row_id = lax.broadcasted_iota(jnp.int32, (WINDOW, PAIR), 0)
    ones = jnp.ones((SPAN, PAIR), jnp.bfloat16)

    def set_bias(valid):
        allowed = (jnp.abs(offset) <= WINDOW) & (valid | (offset == 0))
        bias[...] = jnp.where(allowed, 0.0, -jnp.inf)

    def block(t, carry):
        b = (t + 1) % blocks
        r = pl.multiple_of(b * WINDOW, WINDOW)
        place = lane + (r - WINDOW)

        @pl.when(t < blocks - 2)
        def _():
            set_bias(place < counts[0])

        @pl.when(t == blocks - 2)
        def _():
            @pl.when(has_right)
            def _():
                for copy in to_left:
                    copy.wait_recv()

            @pl.when(jnp.logical_not(has_right))
            def _():
                cnt_near[1] = jnp.zeros(cnt.shape, jnp.int32)
                k[after] = jnp.zeros((WINDOW, width), jnp.bfloat16)
                v[after] = jnp.zeros((WINDOW, width), jnp.bfloat16)

            near = jnp.concatenate([cnt_near[1, 0:1, :]] * 3, axis=1)
            limit = jnp.where(lane[0:1] < 2 * WINDOW, counts[0], near + rows)
            set_bias(place < limit)

        @pl.when(t == blocks - 1)
        def _():
            @pl.when(has_left)
            def _():
                for copy in to_right:
                    copy.wait_recv()

            @pl.when(jnp.logical_not(has_left))
            def _():
                cnt_near[0] = jnp.zeros(cnt.shape, jnp.int32)
                k[before] = jnp.zeros((WINDOW, width), jnp.bfloat16)
                v[before] = jnp.zeros((WINDOW, width), jnp.bfloat16)

            near = jnp.concatenate([cnt_near[0, 0:1, :]] * 3, axis=1)
            limit = jnp.where(lane[0:1] < WINDOW, near - rows, counts[0])
            set_bias(place < limit)

        kept = row_id + r < counts[0]
        for p in range(width // PAIR):
            cols = slice(p * PAIR, (p + 1) * PAIR)
            q_pair = q[pl.ds(r, WINDOW), cols]
            zero = jnp.zeros_like(q_pair)
            stacked = jnp.concatenate(
                [jnp.where(head_a, q_pair, zero), jnp.where(head_a, zero, q_pair)], axis=0
            )
            s = lax.dot_general(
                stacked, k[pl.ds(r, SPAN), cols], NT, preferred_element_type=jnp.float32
            )
            s = s + jnp.concatenate([bias[...], bias[...]], axis=0)
            e = jnp.exp2(s - jnp.max(s, axis=-1, keepdims=True)).astype(jnp.bfloat16)
            wide = jnp.concatenate([v[pl.ds(r, SPAN), cols], ones], axis=1)
            m = jnp.dot(e, wide, preferred_element_type=jnp.float32)
            mixed = jnp.where(head_a, m[:WINDOW, :PAIR], m[WINDOW:, :PAIR])
            total = jnp.where(head_a, m[:WINDOW, PAIR:], m[WINDOW:, PAIR:])
            o[pl.ds(r, WINDOW), cols] = jnp.where(kept, mixed / total, 0.0).astype(jnp.bfloat16)
        pltpu.make_async_copy(
            o.at[pl.ds(r, WINDOW)], out_hbm.at[pl.ds(r, WINDOW)], out_sem.at[b]
        ).start()
        return carry

    lax.fori_loop(0, blocks, block, 0)

    for b in range(blocks):
        part = pl.ds(b * WINDOW, WINDOW)
        pltpu.make_async_copy(o.at[part], out_hbm.at[part], out_sem.at[b]).wait()

    @pl.when(has_right)
    def _():
        for copy in to_right:
            copy.wait_send()

    @pl.when(has_left)
    def _():
        for copy in to_left:
            copy.wait_send()


def local(inputs, counts, query_weight, key_weight, value_weight):
    rows, depth = inputs.shape
    width = query_weight.shape[1]
    bf16 = jnp.bfloat16
    anywhere = pl.BlockSpec(memory_space=pl.ANY)
    macs = rows * width * (3 * depth + 4 * SPAN)
    return pl.pallas_call(
        kernel,
        out_shape=jax.ShapeDtypeStruct((rows, width), bf16),
        in_specs=[pl.BlockSpec(memory_space=pltpu.SMEM)] + [anywhere] * 4,
        out_specs=anywhere,
        scratch_shapes=[
            pltpu.VMEM((rows, depth), bf16),
            pltpu.VMEM((depth, width), bf16),
            pltpu.VMEM((depth, width), bf16),
            pltpu.VMEM((depth, width), bf16),
            pltpu.VMEM((rows, width), bf16),
            pltpu.VMEM((rows + 2 * WINDOW, width), bf16),
            pltpu.VMEM((rows + 2 * WINDOW, width), bf16),
            pltpu.VMEM((rows, width), bf16),
            pltpu.VMEM((WINDOW, SPAN), jnp.float32),
            pltpu.VMEM((8, 128), jnp.int32),
            pltpu.VMEM((2, 8, 128), jnp.int32),
            pltpu.SemaphoreType.DMA((rows // 256,)),
            pltpu.SemaphoreType.DMA((3,)),
            pltpu.SemaphoreType.DMA((rows // WINDOW,)),
            pltpu.SemaphoreType.DMA((6,)),
            pltpu.SemaphoreType.DMA((6,)),
        ],
        compiler_params=pltpu.CompilerParams(
            collective_id=0, has_side_effects=True, vmem_limit_bytes=48 * 1024 * 1024
        ),
        cost_estimate=pl.CostEstimate(
            flops=2 * macs, bytes_accessed=15 * 2**20, transcendentals=rows * SPAN * width // DH
        ),
    )(counts, inputs, query_weight, key_weight, value_weight)


def solution(mesh):
    placed = (P(("groups", "tm"), None), P(("groups", "tm")), P(), P(), P())
    return jax.shard_map(
        local, mesh=mesh, in_specs=placed, out_specs=P(("groups", "tm"), None), check_vma=False
    )
```

profile of v0, /device:TPU:31, one launch (start us, length us, event | category | flops | bytes accessed | tf_op | source)
XLA Modules:
  0.0 38.5 jit_solution(8514943739283651759)
XLA Ops:
  0.7 0.0 copy-start
  0.7 1.9 %copy-done = bf16[1024,1536]{1,0:T(8,128)(2,1)S(1)} copy-done((bf16[1024,1536]{1,0:T(8,128)(2,1)S(1)}, bf16[1024,1536]{1,0:T(8,128)(2,1)}, u32[]{:S(2)}) %copy-start) | copy-done | bytes 3145752
  2.5 34.7 %shard_map.55 = bf16[1024,1024]{1,0:T(8,128)(2,1)S(1)} custom-call(s32[1]{0:T(128)S(6)} %copy.7.counts, bf16[1024,1536]{1,0:T(8,128)(2,1)S(1)} %copy-done, bf16[1536,1024]{1,0:T(8,128)(2,1)} %wq_hbm.1, bf16[1536,1024]{1,0:T(8,128)(2,1)} %wk_hbm.1, bf16[1536,1024]{1,0:T(8,128)(2,1)} %wv_hbm.1), custom_call_target="tpu_custom_call" | custom-call | flops 12884901888 | bytes 15728640 | tf_op jit(solution)/shard_map/pallas_call | solution.py:226
  37.2 1.3 %copy.8 = bf16[1024,1024]{1,0:T(8,128)(2,1)} copy(bf16[1024,1024]{1,0:T(8,128)(2,1)S(1)} %shard_map.55) | data formatting | bytes 4194304
Async XLA Ops:
  0.7 1.9 %copy-start = (bf16[1024,1536]{1,0:T(8,128)(2,1)S(1)}, bf16[1024,1536]{1,0:T(8,128)(2,1)}, u32[]{:S(2)}) copy-start(bf16[1024,1536]{1,0:T(8,128)(2,1)} %x_hbm.1) | copy-start | bytes 9437188
where the time goes:
time: 38.7 us; the launch traced here: 38.5 us
  Pallas kernels  34.7 us (90%)
  local copies, waits for them, and re-layouts  3.2 us (8%)
  between operations  0.67 us (2%)
    pallas_call x1, Pallas kernels, local(): pl.pallas_call(kernel, out_shape=jax.ShapeDtypeStruct((rows, width), bf16...  34.7 us
    unnamed x3, local copies, waits for them, and re-layouts  3.2 us

commit v1 on v0

--- a/solution.py
+++ b/solution.py
@@ -26,7 +26,7 @@
 
 def kernel(
     counts, x_hbm, wq_hbm, wk_hbm, wv_hbm, out_hbm,
-    x, wq, wk, wv, q, k, v, o, bias, cnt, cnt_near,
+    x, wq, wk, wv, q, k, v, o, bias, sb, mb, cnt, cnt_near,
     x_sem, w_sem, out_sem, send_sem, recv_sem,
 ):
     rows, width = out_hbm.shape
@@ -91,11 +91,11 @@
         x_copy[c].wait()
 
         def norm(t, carry, c=c):
-            part = pl.ds(pl.multiple_of(c * chunk + t * 64, 64), 64)
+            part = pl.ds(pl.multiple_of(c * chunk + t * 32, 32), 32)
             x[part] = normalize(x[part])
             return carry
 
-        lax.fori_loop(0, chunk // 64, norm, 0)
+        lax.fori_loop(0, chunk // 32, norm, 0, unroll=True)
 
     def project(w, dst, shift, scale):
         def step(t, carry):
@@ -109,7 +109,7 @@
             dst[to, col] = y.astype(jnp.bfloat16)
             return carry
 
-        lax.fori_loop(0, 2 * (width // 256), step, 0)
+        lax.fori_loop(0, 2 * (width // 256), step, 0, unroll=True)
 
     w_copy[0].wait()
     project(wk, k, WINDOW, 1.0)
@@ -178,7 +178,7 @@
             set_bias(place < limit)
 
         kept = row_id + r < counts[0]
-        for p in range(width // PAIR):
+        def scores(p):
             cols = slice(p * PAIR, (p + 1) * PAIR)
             q_pair = q[pl.ds(r, WINDOW), cols]
             zero = jnp.zeros_like(q_pair)
@@ -188,13 +188,24 @@
             s = lax.dot_general(
                 stacked, k[pl.ds(r, SPAN), cols], NT, preferred_element_type=jnp.float32
             )
-            s = s + jnp.concatenate([bias[...], bias[...]], axis=0)
-            e = jnp.exp2(s - jnp.max(s, axis=-1, keepdims=True)).astype(jnp.bfloat16)
+            return s + jnp.concatenate([bias[...], bias[...]], axis=0)
+
+        def mix(p, e):
+            cols = slice(p * PAIR, (p + 1) * PAIR)
             wide = jnp.concatenate([v[pl.ds(r, SPAN), cols], ones], axis=1)
             m = jnp.dot(e, wide, preferred_element_type=jnp.float32)
             mixed = jnp.where(head_a, m[:WINDOW, :PAIR], m[WINDOW:, :PAIR])
             total = jnp.where(head_a, m[:WINDOW, PAIR:], m[WINDOW:, PAIR:])
             o[pl.ds(r, WINDOW), cols] = jnp.where(kept, mixed / total, 0.0).astype(jnp.bfloat16)
+
+        pairs = width // PAIR
+        for p in range(pairs):
+            s = scores(p)
+            sb[p] = s
+            mb[p] = jnp.broadcast_to(jnp.max(s, axis=-1, keepdims=True), (2 * WINDOW, PAIR))
+        for p in range(pairs):
+            top = jnp.concatenate([mb[p]] * 3, axis=1)
+            mix(p, jnp.exp2(sb[p] - top).astype(jnp.bfloat16))
         pltpu.make_async_copy(
             o.at[pl.ds(r, WINDOW)], out_hbm.at[pl.ds(r, WINDOW)], out_sem.at[b]
         ).start()
@@ -238,6 +249,8 @@
             pltpu.VMEM((rows + 2 * WINDOW, width), bf16),
             pltpu.VMEM((rows, width), bf16),
             pltpu.VMEM((WINDOW, SPAN), jnp.float32),
+            pltpu.VMEM((width // PAIR, 2 * WINDOW, SPAN), jnp.float32),
+            pltpu.VMEM((width // PAIR, 2 * WINDOW, PAIR), jnp.float32),
             pltpu.VMEM((8, 128), jnp.int32),
             pltpu.VMEM((2, 8, 128), jnp.int32),
             pltpu.SemaphoreType.DMA((rows // 256,)),
@@ -247,7 +260,7 @@
             pltpu.SemaphoreType.DMA((6,)),
         ],
         compiler_params=pltpu.CompilerParams(
-            collective_id=0, has_side_effects=True, vmem_limit_bytes=48 * 1024 * 1024
+            collective_id=0, has_side_effects=True, vmem_limit_bytes=50 * 1024 * 1024
         ),
         cost_estimate=pl.CostEstimate(
             flops=2 * macs, bytes_accessed=15 * 2**20, transcendentals=rows * SPAN * width // DH

time: 38.7 us -> 28 us (0.72)
  Pallas kernels: 34.7 us -> 25.9 us
  local copies, waits for them, and re-layouts: 3.2 us -> 1.32 us
    pallas_call x1, Pallas kernels: 34.7 us -> 25.9 us  [local(): pl.pallas_call(kernel, out_shape=jax.ShapeDtypeStruct((rows, width), bf16...]
    unnamed x3 -> x1, local copies, waits for them, and re-layouts: 3.2 us -> 1.32 us
where the time goes in v1:
time: 28 us; the launch traced here: 27.9 us
  Pallas kernels  25.9 us (92%)
  local copies, waits for them, and re-layouts  1.32 us (5%)
  between operations  0.66 us (2%)
    pallas_call x1, Pallas kernels, local(): pl.pallas_call(kernel, out_shape=jax.ShapeDtypeStruct((rows, width), bf16...  25.9 us
    unnamed x1, local copies, waits for them, and re-layouts  1.32 us

profile of v1, /device:TPU:31, one launch (start us, length us, event | category | flops | bytes accessed | tf_op | source)
XLA Modules:
  0.0 27.9 jit_solution(4641970969900460968)
XLA Ops:
  0.7 25.9 %shard_map.55 = bf16[1024,1024]{1,0:T(8,128)(2,1)S(1)} custom-call(s32[1]{0:T(128)S(6)} %copy.7.counts, bf16[1024,1536]{1,0:T(8,128)(2,1)} %x_hbm.1, bf16[1536,1024]{1,0:T(8,128)(2,1)} %wq_hbm.1, bf16[1536,1024]{1,0:T(8,128)(2,1)} %wk_hbm.1, bf16[1536,1024]{1,0:T(8,128)(2,1)} %wv_hbm.1), custom_call_target="tpu_custom_call" | custom-call | flops 12884901888 | bytes 15728640 | tf_op jit(solution)/shard_map/pallas_call | solution.py:237
  26.6 1.3 %copy.8 = bf16[1024,1024]{1,0:T(8,128)(2,1)} copy(bf16[1024,1024]{1,0:T(8,128)(2,1)S(1)} %shard_map.55) | data formatting | bytes 4194304

commit v2 on v1

--- a/solution.py
+++ b/solution.py
@@ -134,9 +134,13 @@
         allowed = (jnp.abs(offset) <= WINDOW) & (valid | (offset == 0))
         bias[...] = jnp.where(allowed, 0.0, -jnp.inf)
 
-    def block(t, carry):
-        b = (t + 1) % blocks
-        r = pl.multiple_of(b * WINDOW, WINDOW)
+    pairs = width // PAIR
+
+    def rows_of(t):
+        return pl.multiple_of(((t + 1) % blocks) * WINDOW, WINDOW)
+
+    def prepare(t):
+        r = rows_of(t)
         place = lane + (r - WINDOW)
 
         @pl.when(t < blocks - 2)
@@ -177,41 +181,54 @@
             limit = jnp.where(lane[0:1] < WINDOW, near - rows, counts[0])
             set_bias(place < limit)
 
+    def scores(t, p):
+        r = rows_of(t)
+        cols = slice(p * PAIR, (p + 1) * PAIR)
+        q_pair = q[pl.ds(r, WINDOW), cols]
+        zero = jnp.zeros_like(q_pair)
+        stacked = jnp.concatenate(
+            [jnp.where(head_a, q_pair, zero), jnp.where(head_a, zero, q_pair)], axis=0
+        )
+        s = lax.dot_general(
+            stacked, k[pl.ds(r, SPAN), cols], NT, preferred_element_type=jnp.float32
+        )
+        s = s + jnp.concatenate([bias[...], bias[...]], axis=0)
+        sb[p] = s
+        mb[p] = jnp.broadcast_to(jnp.max(s, axis=-1, keepdims=True), (2 * WINDOW, PAIR))
+
+    def mix(t, p):
+        r = rows_of(t)
+        cols = slice(p * PAIR, (p + 1) * PAIR)
+        top = jnp.concatenate([mb[p]] * 3, axis=1)
+        e = jnp.exp2(sb[p] - top).astype(jnp.bfloat16)
+        wide = jnp.concatenate([v[pl.ds(r, SPAN), cols], ones], axis=1)
+        m = jnp.dot(e, wide, preferred_element_type=jnp.float32)
+        mixed = jnp.where(head_a, m[:WINDOW, :PAIR], m[WINDOW:, :PAIR])
+        total = jnp.where(head_a, m[:WINDOW, PAIR:], m[WINDOW:, PAIR:])
         kept = row_id + r < counts[0]
-        def scores(p):
-            cols = slice(p * PAIR, (p + 1) * PAIR)
-            q_pair = q[pl.ds(r, WINDOW), cols]
-            zero = jnp.zeros_like(q_pair)
-            stacked = jnp.concatenate(
-                [jnp.where(head_a, q_pair, zero), jnp.where(head_a, zero, q_pair)], axis=0
-            )
-            s = lax.dot_general(
-                stacked, k[pl.ds(r, SPAN), cols], NT, preferred_element_type=jnp.float32
-            )
-            return s + jnp.concatenate([bias[...], bias[...]], axis=0)
-
-        def mix(p, e):
-            cols = slice(p * PAIR, (p + 1) * PAIR)
-            wide = jnp.concatenate([v[pl.ds(r, SPAN), cols], ones], axis=1)
-            m = jnp.dot(e, wide, preferred_element_type=jnp.float32)
-            mixed = jnp.where(head_a, m[:WINDOW, :PAIR], m[WINDOW:, :PAIR])
-            total = jnp.where(head_a, m[:WINDOW, PAIR:], m[WINDOW:, PAIR:])
-            o[pl.ds(r, WINDOW), cols] = jnp.where(kept, mixed / total, 0.0).astype(jnp.bfloat16)
-
-        pairs = width // PAIR
+        o[pl.ds(r, WINDOW), cols] = jnp.where(kept, mixed / total, 0.0).astype(jnp.bfloat16)
+
+    def ship(t):
+        r = rows_of(t)
+        pltpu.make_async_copy(
+            o.at[pl.ds(r, WINDOW)], out_hbm.at[pl.ds(r, WINDOW)], out_sem.at[(t + 1) % blocks]
+        ).start()
+
+    def block(t, carry):
+        prepare(t + 1)
         for p in range(pairs):
-            s = scores(p)
-            sb[p] = s
-            mb[p] = jnp.broadcast_to(jnp.max(s, axis=-1, keepdims=True), (2 * WINDOW, PAIR))
-        for p in range(pairs):
-            top = jnp.concatenate([mb[p]] * 3, axis=1)
-            mix(p, jnp.exp2(sb[p] - top).astype(jnp.bfloat16))
-        pltpu.make_async_copy(
-            o.at[pl.ds(r, WINDOW)], out_hbm.at[pl.ds(r, WINDOW)], out_sem.at[b]
-        ).start()
+            mix(t, p)
+            scores(t + 1, p)
+        ship(t)
         return carry
 
-    lax.fori_loop(0, blocks, block, 0)
+    prepare(0)
+    for p in range(pairs):
+        scores(0, p)
+    lax.fori_loop(0, blocks - 1, block, 0)
+    for p in range(pairs):
+        mix(blocks - 1, p)
+    ship(blocks - 1)
 
     for b in range(blocks):
         part = pl.ds(b * WINDOW, WINDOW)

time: 28 us -> 27.6 us (0.986)
  Pallas kernels: 25.9 us -> 25.4 us
    pallas_call x1, Pallas kernels: 25.9 us -> 25.4 us  [local(): pl.pallas_call(kernel, out_shape=jax.ShapeDtypeStruct((rows, width), bf16...]
where the time goes in v2:
time: 27.6 us; the launch traced here: 27.4 us
  Pallas kernels  25.4 us (92%)
  local copies, waits for them, and re-layouts  1.32 us (5%)
  between operations  0.66 us (2%)
    pallas_call x1, Pallas kernels, local(): pl.pallas_call(kernel, out_shape=jax.ShapeDtypeStruct((rows, width), bf16...  25.4 us
    unnamed x1, local copies, waits for them, and re-layouts  1.32 us

profile of v2, /device:TPU:31, one launch (start us, length us, event | category | flops | bytes accessed | tf_op | source)
XLA Modules:
  0.0 27.4 jit_solution(2745796695527495152)
XLA Ops:
  0.7 25.4 %shard_map.55 = bf16[1024,1024]{1,0:T(8,128)(2,1)S(1)} custom-call(s32[1]{0:T(128)S(6)} %copy.7.counts, bf16[1024,1536]{1,0:T(8,128)(2,1)} %x_hbm.1, bf16[1536,1024]{1,0:T(8,128)(2,1)} %wq_hbm.1, bf16[1536,1024]{1,0:T(8,128)(2,1)} %wk_hbm.1, bf16[1536,1024]{1,0:T(8,128)(2,1)} %wv_hbm.1), custom_call_target="tpu_custom_call" | custom-call | flops 12884901888 | bytes 15728640 | tf_op jit(solution)/shard_map/pallas_call | solution.py:254
  26.1 1.3 %copy.8 = bf16[1024,1024]{1,0:T(8,128)(2,1)} copy(bf16[1024,1024]{1,0:T(8,128)(2,1)S(1)} %shard_map.55) | data formatting | bytes 4194304
